TPU v7x, 128 devices: a whole 4x4x4 slice. The times are simulated.
128 devices in a mesh: group: 8 (over x, core), tile: 16 (over y, z).
Axes of the slice: x: 4, y: 4, z: 4, core: 2. Of those that a mesh axis runs over, the one named last changes fastest.
Arguments:
- image: bfloat16 [8, 192, 48, 512], P('group', 'tile'), may hold values from -6 to 6
- grad_out: bfloat16 [8, 192, 48, 512], P('group', 'tile'), may hold values from -6 to 6
- gate: bfloat16 [8, 192, 48], P('group', 'tile'), may hold values from 0.19921875 to 1
- routes: int32 [8, 192, 48, 1], P('group', 'tile'), may hold values from 0 to 15; in each aligned block of 576 rows (0 to 575, 576 to 1151, ..., all dimensions but the last counted through in order) at most 72 rows name the same one
- gain_one: float32 [512], replicated, may hold values from 0.1 to 1.9
- w_qkv: bfloat16 [512, 1536], replicated, may hold values from -0.25 to 0.25
- w_proj: bfloat16 [512, 512], replicated, may hold values from -0.25 to 0.25
- table: float32 [16, 529], replicated, may hold values from -4 to 303
- gain_two: float32 [512], replicated, may hold values from 0.1 to 1.9
- w_fc1: bfloat16 [16, 512, 2048], P('tile'), may hold values from -0.25 to 0.25
- w_fc2: bfloat16 [16, 2048, 512], P('tile'), may hold values from -0.125 to 0.125
Outputs:
- grad_image: bfloat16 [8, 192, 48, 512], P('group', 'tile')
- grad_gate: float32 [8, 192, 48], P('group', 'tile')
- grad_fc1: float32 [16, 512, 2048], P('tile')
- grad_fc2: float32 [16, 2048, 512], P('tile')
- grad_qkv: float32 [512, 1536], replicated
- grad_proj: float32 [512, 512], replicated
- grad_table: float32 [16, 529], replicated
- grad_gain_one: float32 [512], replicated
- grad_gain_two: float32 [512], replicated
Inputs may be any that keep to these rules, and one draw needn't show every extreme that they name: `routes`: among the 576 tokens of one image in one band of 12 rows (one tile), no expert is named more than 72 times.
All inputs are finite; a program needn't handle non-finite values.
Results may differ from a plain program's by a relative error of at most 0.035.
Values may be sent and summed in bfloat16 or wider, within the bound.
No kernel may reach another device: no remote copies, remote signals or barrier semaphores. Data moves between devices by JAX's collectives and lax.ppermute only.
A program may use at most 192 MiB of HBM per device.

v0:
```python
import functools

import jax
import jax.numpy as jnp
import numpy as np
from jax import lax
from jax.sharding import PartitionSpec as P

HEADS = 16
WINDOW = 12
SHIFT = 6


def shifted(value, axis, steps):
    count = lax.axis_size(axis)
    pairs = [(source, (source + steps) % count) for source in range(count)]
    return lax.ppermute(value, axis, pairs)


def shortened(value):
    return jax.tree.map(lambda a: a.astype(jnp.bfloat16) if a.dtype == jnp.float32 else a, value)


def relative_index(window):
    grid_rows, grid_cols = np.meshgrid(np.arange(window), np.arange(window), indexing="ij")
    flat_r = grid_rows.reshape(-1)
    flat_c = grid_cols.reshape(-1)
    delta_r = flat_r[:, None] - flat_r[None, :] + window - 1
    delta_c = flat_c[:, None] - flat_c[None, :] + window - 1
    return (delta_r * (2 * window - 1) + delta_c).astype(np.int32)


def layer_norm(values, gain_vec):
    row_mean = jnp.mean(values, axis=-1, keepdims=True)
    centred = values - row_mean
    row_var = jnp.mean(centred * centred, axis=-1, keepdims=True)
    return centred * lax.rsqrt(row_var + 1e-05) * gain_vec


def gelu_exact(values):
    return 0.5 * values * (1.0 + jax.scipy.special.erf(values * 0.7071067811865476))


def gelu_slope(values):
    cumulative = 0.5 * (1.0 + jax.scipy.special.erf(values * 0.7071067811865476))
    density = jnp.exp(-0.5 * values * values) * 0.3989422804014327
    return cumulative + values * density


def window_masks(row_last, col_windows):
    inner_pos = jnp.arange(WINDOW * WINDOW, dtype=jnp.int32)
    row_in = inner_pos // WINDOW
    col_in = inner_pos % WINDOW
    row_region = jnp.where(row_last[:, None], jnp.where(row_in < SHIFT, 1, 2)[None], 0)
    col_last = jnp.arange(col_windows, dtype=jnp.int32) == col_windows - 1
    col_region = jnp.where(col_last[:, None], jnp.where(col_in < SHIFT, 1, 2)[None], 0)
    region = (row_region[:, None, :] * 3 + col_region[None, :, :]).reshape(-1, WINDOW * WINDOW)
    same = region[:, :, None] == region[:, None, :]
    return jnp.where(same, 0.0, -100.0).astype(jnp.float32)


def to_windows(field_in):
    row_count, col_count, channels = field_in.shape
    blocks = field_in.reshape(row_count // WINDOW, WINDOW, col_count // WINDOW, WINDOW, channels)
    return blocks.transpose(0, 2, 1, 3, 4).reshape(-1, WINDOW * WINDOW, channels)


def from_windows(windows, row_count, col_count):
    channels = windows.shape[-1]
    blocks = windows.reshape(row_count // WINDOW, col_count // WINDOW, WINDOW, WINDOW, channels)
    return blocks.transpose(0, 2, 1, 3, 4).reshape(row_count, col_count, channels)


def core_attention(qkv_act, table, mask_add):
    win_count, win_tokens, triple = qkv_act.shape
    channels = triple // 3
    head_dim = channels // HEADS
    split_qkv = qkv_act.reshape(win_count, win_tokens, 3, HEADS, head_dim)
    logits = jnp.einsum(
        "nqhd,nkhd->nhqk",
        split_qkv[:, :, 0],
        split_qkv[:, :, 1],
        preferred_element_type=jnp.float32,
    ) * head_dim ** (-0.5)
    rel_bias = jnp.take(table, relative_index(WINDOW), axis=1)
    logits = logits + rel_bias[None] + mask_add[:, None]
    attn_prob = jax.nn.softmax(logits, axis=-1).astype(jnp.bfloat16)
    mixed_heads = jnp.einsum(
        "nhqk,nkhd->nqhd", attn_prob, split_qkv[:, :, 2], preferred_element_type=jnp.float32
    )
    return mixed_heads.astype(jnp.bfloat16).reshape(win_count, win_tokens, channels)


def attend_forward(windows, mask_add, gain_one, w_qkv, w_proj, table):
    window_shape = windows.shape
    flat_rows = windows.reshape(-1, window_shape[2]).astype(jnp.float32)
    normed_f, norm_pull = jax.vjp(layer_norm, flat_rows, gain_one)
    normed = normed_f.astype(jnp.bfloat16)
    qkv_act = jnp.dot(normed, w_qkv, preferred_element_type=jnp.float32).astype(jnp.bfloat16)
    qkv_act = qkv_act.reshape(window_shape[0], window_shape[1], -1)
    mixed_heads, core_pull = jax.vjp(
        functools.partial(core_attention, mask_add=mask_add), qkv_act, table
    )
    mixed_rows = mixed_heads.reshape(flat_rows.shape[0], -1)
    residual_sum = flat_rows + jnp.dot(mixed_rows, w_proj, preferred_element_type=jnp.float32)
    return (residual_sum, (normed, mixed_rows, norm_pull, core_pull, window_shape))


def attend_backward(stored, cotangent, w_qkv, w_proj):
    normed, mixed_rows, norm_pull, core_pull, window_shape = stored
    cot_half = cotangent.astype(jnp.bfloat16)
    grad_mixed = jnp.dot(cot_half, w_proj.T, preferred_element_type=jnp.float32).astype(
        jnp.bfloat16
    )
    grad_qkv_act, grad_table = core_pull(grad_mixed.reshape(window_shape))
    grad_qkv_act = grad_qkv_act.reshape(normed.shape[0], -1)
    grad_normed = jnp.dot(grad_qkv_act, w_qkv.T, preferred_element_type=jnp.float32)
    grad_rows, grad_gain = norm_pull(grad_normed)
    result_rows = cotangent + grad_rows
    grad_proj = jnp.dot(mixed_rows.T, cot_half, preferred_element_type=jnp.float32)
    grad_qkv = jnp.dot(normed.T, grad_qkv_act, preferred_element_type=jnp.float32)
    return (result_rows, (grad_gain, grad_qkv, grad_proj, grad_table))


def expert_pass(block_in, block_grad, block_gate, w_up, w_down):
    pre_act = jnp.dot(block_in, w_up, preferred_element_type=jnp.float32)
    hidden = gelu_exact(pre_act).astype(jnp.bfloat16)
    output = jnp.dot(hidden, w_down, preferred_element_type=jnp.float32)
    grad_output = (block_gate.astype(jnp.float32)[:, None] * block_grad.astype(jnp.float32)).astype(
        jnp.bfloat16
    )
    grad_hidden = jnp.dot(grad_output, w_down.T, preferred_element_type=jnp.float32)
    grad_pre = (grad_hidden * gelu_slope(pre_act)).astype(jnp.bfloat16)
    grad_down = jnp.dot(hidden.T, grad_output, preferred_element_type=jnp.float32)
    grad_up = jnp.dot(block_in.T, grad_pre, preferred_element_type=jnp.float32)
    grad_inputs = jnp.dot(grad_pre, w_up.T, preferred_element_type=jnp.float32).astype(jnp.bfloat16)
    return (grad_inputs, output, grad_up, grad_down)


def dispatch_table(route_flat, experts, capacity):
    token_count = route_flat.shape[0]
    expert_ids = jnp.arange(experts, dtype=jnp.int32)
    onehot = (route_flat[:, None] == expert_ids[None]).astype(jnp.bfloat16)
    order_ids = jnp.arange(token_count, dtype=jnp.int32)
    lower = (order_ids[:, None] >= order_ids[None, :]).astype(jnp.bfloat16)
    running = jnp.dot(lower, onehot, preferred_element_type=jnp.float32)
    slot_in = jnp.sum(running * onehot.astype(jnp.float32), axis=1) - 1.0
    positions = route_flat * capacity + slot_in.astype(jnp.int32)
    slot_ids = jnp.arange(experts * capacity, dtype=jnp.int32)
    return positions[:, None] == slot_ids[None]


def on_device(
    image, grad_out, gate, routes, gain_one, w_qkv, w_proj, table, gain_two, w_fc1, w_fc2
):
    tile_count = lax.axis_size("tile")
    tile_index = lax.axis_index("tile")
    strip_height = image.shape[1]
    columns = image.shape[2]
    channels = image.shape[3]
    col_windows = columns // WINDOW
    rows_dev = strip_height * columns
    capacity = 2 * rows_dev // tile_count
    below = shifted(image[:, :SHIFT], "tile", -1)[0]
    band = jnp.concatenate([image[0, SHIFT:], below], axis=0)
    mask_add = window_masks(jnp.reshape(tile_index == tile_count - 1, (1,)), col_windows)
    windows = to_windows(jnp.roll(band, -SHIFT, axis=1))
    residual_sum, stored = attend_forward(windows, mask_add, gain_one, w_qkv, w_proj, table)
    attended = jnp.roll(
        from_windows(residual_sum.reshape(windows.shape), WINDOW, columns), SHIFT, axis=1
    )
    upper = shifted(attended[SHIFT:].astype(jnp.bfloat16), "tile", 1).astype(jnp.float32)
    after_attn = jnp.concatenate([upper, attended[:SHIFT]], axis=0)
    tokens = after_attn.reshape(rows_dev, channels)
    normed_f, norm_pull = jax.vjp(layer_norm, tokens, gain_two)
    inputs = normed_f.astype(jnp.bfloat16)
    route_flat = routes.reshape(rows_dev)
    matches = dispatch_table(route_flat, tile_count, capacity)
    dispatch = matches.astype(jnp.bfloat16)
    dispatch_wide = matches.astype(jnp.float32)
    grad_rows_out = grad_out.reshape(rows_dev, channels)
    send_in = jnp.dot(dispatch.T, inputs, preferred_element_type=jnp.float32).astype(jnp.bfloat16)
    send_grad = jnp.dot(dispatch.T, grad_rows_out, preferred_element_type=jnp.float32).astype(
        jnp.bfloat16
    )
    send_gate = (
        jnp.dot(gate.reshape(1, rows_dev), dispatch, preferred_element_type=jnp.float32)
        .astype(jnp.bfloat16)
        .reshape(-1)
    )
    recv_in, recv_grad, recv_gate = (
        lax.all_to_all(send_in, "tile", split_axis=0, concat_axis=0, tiled=True),
        lax.all_to_all(send_grad, "tile", split_axis=0, concat_axis=0, tiled=True),
        lax.all_to_all(send_gate, "tile", split_axis=0, concat_axis=0, tiled=True),
    )
    grad_inputs, output, grad_up, grad_down = expert_pass(
        recv_in, recv_grad, recv_gate, w_fc1[0], w_fc2[0]
    )
    back_inputs = lax.all_to_all(grad_inputs, "tile", split_axis=0, concat_axis=0, tiled=True)
    back_outputs = lax.all_to_all(
        output.astype(jnp.bfloat16), "tile", split_axis=0, concat_axis=0, tiled=True
    ).astype(output.dtype)
    picked = jnp.dot(dispatch_wide, back_outputs, precision=lax.Precision.HIGHEST)
    grad_gate = jnp.sum(grad_rows_out.astype(jnp.float32) * picked, axis=1)
    token_grads = jnp.dot(dispatch, back_inputs, preferred_element_type=jnp.float32)
    grad_tokens, grad_gain_two = norm_pull(token_grads)
    grad_after = (grad_rows_out.astype(jnp.float32) + grad_tokens).reshape(
        strip_height, columns, channels
    )
    grad_below = shifted(shortened(grad_after[:SHIFT]), "tile", -1)
    cot_band = jnp.concatenate([grad_after[SHIFT:], grad_below], axis=0)
    cot_windows = to_windows(jnp.roll(cot_band, -SHIFT, axis=1))
    grad_rows, weight_grads = attend_backward(
        stored, cot_windows.reshape(-1, channels), w_qkv, w_proj
    )
    grad_band = jnp.roll(
        from_windows(grad_rows.reshape(cot_windows.shape), WINDOW, columns), SHIFT, axis=1
    )
    grad_upper = shifted(shortened(grad_band[SHIFT:]), "tile", 1)
    grad_image = jnp.concatenate([grad_upper, grad_band[:SHIFT]], axis=0).astype(jnp.bfloat16)
    summed_up, summed_down = (
        lax.psum(grad_up.astype(jnp.bfloat16), "group").astype(jnp.float32),
        lax.psum(grad_down.astype(jnp.bfloat16), "group").astype(jnp.float32),
    )
    shared_total = lax.psum(
        (weight_grads[0], weight_grads[1], weight_grads[2], weight_grads[3], grad_gain_two),
        ("group", "tile"),
    )
    return (
        grad_image.reshape(1, strip_height, columns, channels),
        grad_gate.reshape(1, strip_height, columns),
        summed_up.reshape(1, channels, -1),
        summed_down.reshape(1, -1, channels),
        shared_total[1],
        shared_total[2],
        shared_total[3],
        shared_total[0],
        shared_total[4],
    )


def solution(mesh):
    return jax.shard_map(
        on_device,
        mesh=mesh,
        in_specs=(
            P("group", "tile", None, None),
            P("group", "tile", None, None),
            P("group", "tile", None),
            P("group", "tile", None, None),
            P(),
            P(),
            P(),
            P(),
            P(),
            P("tile", None, None),
            P("tile", None, None),
        ),
        out_specs=(
            P("group", "tile", None, None),
            P("group", "tile", None),
            P("tile", None, None),
            P("tile", None, None),
            P(),
            P(),
            P(),
            P(),
            P(),
        ),
        check_vma=False,
    )
```

profile of v0, /device:TPU:1, one launch (start us, length us, event | category | flops | bytes accessed | tf_op | source)
XLA Modules:
  0.0 533.1 jit_solution(9977998211718673108)
XLA Ops:
  10.5 8.6 %all-to-all-start = ((bf16[16,72,1]{1,2,0:T(2,128)(2,1)}), bf16[16,72,1]{1,2,0:T(2,128)(2,1)}, u32[]{:S(2)}, u32[]{:S(2)}) async-start(bf16[16,72,1]{1,2,0:T(2,128)(2,1)} %all_to_all.49), calls=%async_computation | async-start | bytes 16384 | tf_op jit(solution)/shard_map/all_to_all | solution.py:194
  19.3 4.7 collective-permute-start
  25.0 38.8 %gather_fusion = f32[20736,16]{1,0:T(8,128)} fusion(f32[16,529]{0,1:T(8,128)S(1)} %copy.117, s32[21504]{0:T(1024)S(1)} %pad_clamp_fusion), kind=kCustom, calls=%fused_computation | custom fusion | bytes 2737152 | tf_op jit(solution)/shard_map/jvp(jit(_take))/gather | solution.py:85
  63.9 12.2 %copy.118 = f32[144,144,16]{0,1,2:T(8,128)} copy(f32[144,144,16]{2,1,0:T(8,128)} %bitcast.138) | data formatting | bytes 2654208 | tf_op jit(solution)/shard_map/jvp(jit(_take))/gather | solution.py:85
  87.8 4.2 convolution_convert_fusion
  95.9 7.6 %reshape_reshape.16 = bf16[4,144,3,16,32]{1,0,4,3,2:T(4,128)(2,1)} reshape(bf16[576,1536]{0,1:T(8,128)(2,1)} %copy.113) | data formatting | bytes 3538944 | tf_op jit(solution)/shard_map/jvp()/reshape;reshape | solution.py:78
  103.5 4.8 fusion.92
  108.3 9.8 %fusion.94 = (f32[4,16,144]{2,1,0:T(8,128)S(1)}, f32[4,16,144,144]{2,3,1,0:T(8,128)}) fusion(f32[4,144,144]{1,2,0:T(8,128)} %compare_select_fusion, f32[16,144,144]{1,2,0:T(8,128)} %bitcast.150, bf16[4,144,1,16,32]{1,0,4,3,2:T(4,128)(2,1)} %get-tuple-element.72, bf16[4,144,1,16,32]{1,0,4,3,2:T(4,128)(2,1)} %get-tuple-element.73), kind=kOutput, calls=%fused_computation.165 | convolution fusion | flops 91570320 | bytes 8183808 | tf_op jit(solution)/shard_map/jvp()/sub | solution.py:87
  118.2 5.0 divide_convert_fusion
  143.4 6.0 %all-to-all-start.1 = ((bf16[16,72,512]{2,1,0:T(8,128)(2,1)}), bf16[16,72,512]{2,1,0:T(8,128)(2,1)}, u32[]{:S(2)}, u32[]{:S(2)}) async-start(bf16[16,72,512]{2,1,0:T(8,128)(2,1)} %bitcast.153), calls=%async_computation.1 | async-start | bytes 2359296 | tf_op jit(solution)/shard_map/all_to_all | solution.py:193
  157.9 7.8 %all-to-all-done.1 = bf16[16,72,512]{2,1,0:T(8,128)(2,1)} async-done(((bf16[16,72,512]{2,1,0:T(8,128)(2,1)}), bf16[16,72,512]{2,1,0:T(8,128)(2,1)}, u32[]{:S(2)}, u32[]{:S(2)}) %all-to-all-start.1) | async-done | bytes 1179680 | tf_op jit(solution)/shard_map/all_to_all | solution.py:193
  165.7 4.4 all-to-all-start.2
  180.0 5.5 %all-to-all-done.2 = bf16[16,72,512]{2,1,0:T(8,128)(2,1)} async-done(((bf16[16,72,512]{2,1,0:T(8,128)(2,1)}), bf16[16,72,512]{2,1,0:T(8,128)(2,1)}, u32[]{:S(2)}, u32[]{:S(2)}) %all-to-all-start.2) | async-done | bytes 1179680 | tf_op jit(solution)/shard_map/all_to_all | solution.py:192
  185.5 6.0 %multiply_convert_fusion = (bf16[1152,2048]{1,0:T(8,128)(2,1)}, f32[1152,2048]{1,0:T(8,128)S(1)}) fusion(bf16[1152,512]{1,0:T(8,128)(2,1)} %bitcast.17, bf16[1,512,2048]{2,1,0:T(8,128)(2,1)S(1)} %copy-done), kind=kOutput, calls=%fused_computation.15 | convolution fusion | flops 2427715584 | bytes 17432576 | tf_op jit(solution)/shard_map/dot_general | solution.py:126
  191.5 5.5 %fusion.13 = bf16[1152,2048]{1,0:T(8,128)(2,1)S(1)} fusion(f32[1152,2048]{1,0:T(8,128)S(1)} %get-tuple-element.88, bf16[1152,512]{1,0:T(8,128)(2,1)S(1)} %bitcast.156, bf16[1,2048,512]{2,1,0:T(8,128)(2,1)S(1)} %copy-done.49), kind=kOutput, calls=%fused_computation.24 | convolution fusion | flops 2439512064 | bytes 17432576 | tf_op jit(solution)/shard_map/dot_general | solution.py:132
  200.7 5.6 %all-to-all-start.3 = ((bf16[16,72,512]{2,1,0:T(8,128)(2,1)}), bf16[16,72,512]{2,1,0:T(8,128)(2,1)S(1)}, u32[]{:S(2)}, u32[]{:S(2)}) async-start(bf16[16,72,512]{2,1,0:T(8,128)(2,1)} %bitcast.157), calls=%async_computation.3 | async-start | bytes 2359296 | tf_op jit(solution)/shard_map/all_to_all | solution.py:199
  206.3 7.1 %fusion.22 = bf16[1,512,2048]{2,1,0:T(8,128)(2,1)} fusion(bf16[1152,512]{1,0:T(8,128)(2,1)} %bitcast.17, bf16[1152,2048]{1,0:T(8,128)(2,1)} %copy-done.51), kind=kOutput, calls=%fused_computation.41 | convolution fusion | flops 2416967680 | bytes 7995392 | tf_op jit(solution)/shard_map/dot_general | solution.py:135
  213.4 6.0 %convolution_convert_fusion.5 = bf16[1152,512]{1,0:T(8,128)(2,1)} fusion(bf16[1152,2048]{1,0:T(8,128)(2,1)} %get-tuple-element.87, bf16[1,2048,512]{2,1,0:T(8,128)(2,1)S(1)} %copy-done.50), kind=kOutput, calls=%fused_computation.37 | convolution fusion | flops 2416508928 | bytes 7995392 | tf_op jit(solution)/shard_map/dot_general | solution.py:128
  222.1 5.2 all-to-all-start.4
  232.8 4.7 collective-permute-start.2
  237.5 6.6 %fusion.23 = bf16[1,2048,512]{2,1,0:T(8,128)(2,1)} fusion(bf16[1152,2048]{1,0:T(8,128)(2,1)} %get-tuple-element.87, bf16[1152,512]{1,0:T(8,128)(2,1)S(1)} %copy-done.24), kind=kOutput, calls=%fused_computation.42 | convolution fusion | flops 2416967680 | bytes 7995392 | tf_op jit(solution)/shard_map/dot_general | solution.py:134
  257.3 6.6 %fusion.4 = (f32[4,16,144]{2,1,0:T(8,128)S(1)}, bf16[4,16,144,144]{2,3,1,0:T(8,128)(2,1)S(1)}) fusion(f32[4,16,144,144]{2,3,1,0:T(8,128)} %get-tuple-element.81, f32[4,16,144]{2,1,0:T(8,128)S(1)} %multiply_divide_fusion, bf16[4,144,1,16,32]{1,0,4,3,2:T(4,128)(2,1)} %get-tuple-element.71, bf16[4,16,32,144]{3,0,2,1:T(4,128)(2,1)} %bitcast.143), kind=kOutput, calls=%fused_computation.10 | convolution fusion | flops 91560960 | bytes 9216000 | tf_op jit(solution)/shard_map/transpose(jvp(nhqk,nkhd->nqhd))/dot_general | solution.py:88
  266.0 7.1 %fusion.42 = bf16[4,144,1,16,32]{1,4,3,0,2:T(8,128)(2,1)} fusion(bf16[4,144,1,16,32]{1,0,4,3,2:T(4,128)(2,1)S(1)} %copy-done.29, f32[4,16,144,144]{2,3,1,0:T(8,128)} %get-tuple-element.81, bf16[4,16,144,144]{2,3,1,0:T(8,128)(2,1)S(1)} %get-tuple-element.85, f32[4,16,144]{2,1,0:T(8,128)S(1)} %neg.13, f32[4,16,144]{2,1,0:T(8,128)S(1)} %get-tuple-element.80), kind=kOutput, calls=%fused_computation.70 | convolution fusion | flops 91865088 | bytes 9216000 | tf_op jit(solution)/shard_map/transpose(jvp(nqhd,nkhd->nhqk))/dot_general | solution.py:79
  273.2 8.6 %fusion.45 = bf16[4,144,1,16,32]{1,4,3,0,2:T(8,128)(2,1)} fusion(bf16[4,144,1,16,32]{1,0,4,3,2:T(4,128)(2,1)S(1)} %copy-done.28, f32[4,16,144,144]{2,3,1,0:T(8,128)} %get-tuple-element.81, bf16[4,16,144,144]{2,3,1,0:T(8,128)(2,1)} %copy-done.4, f32[4,16,144]{2,1,0:T(8,128)S(1)} %neg.13, f32[4,16,144]{2,1,0:T(8,128)S(1)} %get-tuple-element.80), kind=kOutput, calls=%fused_computation.71 | convolution fusion | flops 91865088 | bytes 9216000 | tf_op jit(solution)/shard_map/transpose(jvp(nqhd,nkhd->nhqk))/dot_general | solution.py:79
  286.5 4.9 copy.130
  291.5 6.5 %reshape.417 = bf16[576,1536]{0,1:T(8,128)(2,1)} reshape(bf16[4,144,3,16,32]{1,0,4,3,2:T(4,128)(2,1)} %copy.130) | data formatting | bytes 3538944 | tf_op jit(solution)/shard_map/reshape;transpose(jvp())/reshape | solution.py:116
  311.5 9.0 %fusion.86 = f32[16,144,144]{1,2,0:T(8,128)} fusion(f32[4,16,144,144]{2,3,1,0:T(8,128)} %get-tuple-element.81, f32[4,16,144]{2,1,0:T(8,128)S(1)} %neg.13, f32[4,16,144]{2,1,0:T(8,128)S(1)} %get-tuple-element.80, bf16[4,16,144,144]{2,3,1,0:T(8,128)(2,1)} %copy-done.4), kind=kLoop, calls=%fused_computation.159 | loop fusion | flops 6303744 | bytes 9363456 | tf_op jit(solution)/shard_map/transpose(jvp())/reduce_sum | solution.py:86
  320.5 11.1 %copy.141 = f32[144,144,16]{2,1,0:T(8,128)} copy(f32[144,144,16]{0,1,2:T(8,128)} %bitcast.142) | data formatting | bytes 2654208 | tf_op jit(solution)/shard_map/transpose(jvp())/reduce_sum | solution.py:86
  331.6 112.5 %scatter_custom_fusion = f32[16,529]{0,1:T(8,128)S(1)} fusion(s32[20736]{0:T(1024)} %constant.115, f32[20736,16]{1,0:T(8,128)} %bitcast.141, f32[]{:T(128)} %constant.29.clone.1), kind=kCustom, calls=%fused_computation.123 | custom fusion | flops 331776 | bytes 34368 | tf_op jit(solution)/shard_map/transpose(jvp(jit(_take)))/scatter-add | solution.py:85
  444.0 68.3 %all-reduce.3 = (f32[16,529]{0,1:T(8,128)S(1)}, f32[512]{0:T(512)}, f32[512]{0:T(512)}) all-reduce(f32[16,529]{0,1:T(8,128)S(1)} %scatter_custom_fusion, f32[512]{0:T(512)S(1)} %get-tuple-element.56, f32[512]{0:T(512)S(1)} %get-tuple-element.54), channel_id=1, replica_groups=mesh['group'=8,'tile'=16] {'group','tile'}, use_global_device_ids=true, to_apply=%region_19.20 | all-reduce | flops 9488 | bytes 75904 | tf_op jit(solution)/shard_map/psum | solution.py:225
  514.0 4.3 reshape.421
  520.9 3.9 copy.185
  (224 shorter events, 108.7 us)
Async XLA Ops:
  7.2 178.3 %copy-start = (bf16[1,512,2048]{2,1,0:T(8,128)(2,1)S(1)}, bf16[1,512,2048]{2,1,0:T(8,128)(2,1)}, u32[]{:S(2)}) copy-start(bf16[1,512,2048]{2,1,0:T(8,128)(2,1)} %param.21) | copy-start | bytes 6291460
  7.2 16.8 %copy-start.39 = (s32[20736]{0:T(1024)S(1)}, s32[20736]{0:T(1024)}, u32[]{:S(2)}) copy-start(s32[20736]{0:T(1024)} %constant.115) | copy-start | bytes 248836
  7.2 12.0 %copy-start.34 = (bf16[1,12,48,512]{3,2,1,0:T(8,128)(2,1)S(1)}, bf16[1,12,48,512]{3,2,1,0:T(8,128)(2,1)}, u32[]{:S(2)}) copy-start(bf16[1,12,48,512]{3,2,1,0:T(8,128)(2,1)} %param.12) | copy-start | bytes 1769476
  9.2 14.8 %copy-start.46 = (s32[576]{0:T(1024)}, s32[576]{0:T(1024)S(1)}, u32[]{:S(2)}) copy-start(s32[576]{0:T(1024)S(1)} %convert_add_fusion.1) | copy-start | bytes 6916
  10.5 132.8 %all-to-all-start = ((bf16[16,72,1]{1,2,0:T(2,128)(2,1)}), bf16[16,72,1]{1,2,0:T(2,128)(2,1)}, u32[]{:S(2)}, u32[]{:S(2)}) async-start(bf16[16,72,1]{1,2,0:T(2,128)(2,1)} %all_to_all.49), calls=%async_computation | async-start | bytes 16384 | tf_op jit(solution)/shard_map/all_to_all | solution.py:194
  19.3 57.8 %copy-start.17 = (bf16[6,48,512]{2,1,0:T(8,128)(2,1)}, bf16[6,48,512]{2,1,0:T(8,128)(2,1)S(1)}, u32[]{:S(2)}) copy-start(bf16[6,48,512]{2,1,0:T(8,128)(2,1)S(1)} %get-tuple-element.76) | copy-start | bytes 884740
  19.3 57.7 %collective-permute-start = (bf16[1,6,48,512]{3,2,1,0:T(8,128)(2,1)S(1)}, bf16[1,6,48,512]{3,2,1,0:T(8,128)(2,1)S(1)}, u32[]{:S(2)}, u32[]{:S(2)}) collective-permute-start(bf16[1,6,48,512]{3,2,1,0:T(8,128)(2,1)S(1)} %get-tuple-element.77), channel_id=1, source_target_pairs={{0,15},{1,0},{2,1},{3,2},{4,3},{5,4},{6,5},{7,6},{8,7},{9,8},{10,9... | collective-permute-start | bytes 884744 | tf_op jit(solution)/shard_map/ppermute | solution.py:17
  87.8 42.4 %copy-start.6 = (f32[576,512]{1,0:T(8,128)}, f32[576,512]{1,0:T(8,128)S(1)}, u32[]{:S(2)}) copy-start(f32[576,512]{1,0:T(8,128)S(1)} %reshape.425) | copy-start | bytes 3538948
  140.5 11.0 %collective-permute-start.1 = (bf16[6,48,512]{2,1,0:T(8,128)(2,1)}, bf16[6,48,512]{2,1,0:T(8,128)(2,1)}, u32[]{:S(2)}, u32[]{:S(2)}) collective-permute-start(bf16[6,48,512]{2,1,0:T(8,128)(2,1)} %fusion.63), channel_id=1, source_target_pairs={{0,1},{1,2},{2,3},{3,4},{4,5},{5,6},{6,7},{7,8},{8,9},{9,10},{10,1... | collective-permute-start | bytes 884744 | tf_op jit(solution)/shard_map/ppermute | solution.py:17
  143.4 22.3 %all-to-all-start.1 = ((bf16[16,72,512]{2,1,0:T(8,128)(2,1)}), bf16[16,72,512]{2,1,0:T(8,128)(2,1)}, u32[]{:S(2)}, u32[]{:S(2)}) async-start(bf16[16,72,512]{2,1,0:T(8,128)(2,1)} %bitcast.153), calls=%async_computation.1 | async-start | bytes 2359296 | tf_op jit(solution)/shard_map/all_to_all | solution.py:193
  157.9 12.3 %copy-start.37 = (f32[4,12,12]{2,0,1:T(4,128)S(1)}, f32[4,12,12]{2,0,1:T(4,128)}, u32[]{:S(2)}) copy-start(f32[4,12,12]{2,0,1:T(4,128)} %copy-done.36) | copy-start | bytes 6916
  157.9 12.3 %copy-start.38 = (f32[4,12,12]{2,0,1:T(4,128)S(1)}, f32[4,12,12]{2,0,1:T(4,128)}, u32[]{:S(2)}) copy-start(f32[4,12,12]{2,0,1:T(4,128)} %get-tuple-element.78) | copy-start | bytes 6916
  157.9 12.3 %copy-start.45 = (f32[512]{0:T(512)S(1)}, f32[512]{0:T(512)}, u32[]{:S(2)}) copy-start(f32[512]{0:T(512)} %param.16) | copy-start | bytes 6148
  165.7 19.8 %all-to-all-start.2 = ((bf16[16,72,512]{2,1,0:T(8,128)(2,1)}), bf16[16,72,512]{2,1,0:T(8,128)(2,1)}, u32[]{:S(2)}, u32[]{:S(2)}) async-start(bf16[16,72,512]{2,1,0:T(8,128)(2,1)} %bitcast.154), calls=%async_computation.2 | async-start | bytes 2359296 | tf_op jit(solution)/shard_map/all_to_all | solution.py:192
  185.5 6.0 %copy-start.26 = (bf16[16,72,512]{2,1,0:T(8,128)(2,1)S(1)}, bf16[16,72,512]{2,1,0:T(8,128)(2,1)}, u32[]{:S(2)}) copy-start(bf16[16,72,512]{2,1,0:T(8,128)(2,1)} %multiply_convert_fusion.1) | copy-start | bytes 3538948
  185.5 6.0 %copy-start.49 = (bf16[1,2048,512]{2,1,0:T(8,128)(2,1)S(1)}, bf16[1,2048,512]{2,1,0:T(8,128)(2,1)}, u32[]{:S(2)}) copy-start(bf16[1,2048,512]{2,1,0:T(8,128)(2,1)} %param.22) | copy-start | bytes 6291460
  200.7 21.4 %all-to-all-start.3 = ((bf16[16,72,512]{2,1,0:T(8,128)(2,1)}), bf16[16,72,512]{2,1,0:T(8,128)(2,1)S(1)}, u32[]{:S(2)}, u32[]{:S(2)}) async-start(bf16[16,72,512]{2,1,0:T(8,128)(2,1)} %bitcast.157), calls=%async_computation.3 | async-start | bytes 2359296 | tf_op jit(solution)/shard_map/all_to_all | solution.py:199
  206.3 7.1 %copy-start.50 = (bf16[1,2048,512]{2,1,0:T(8,128)(2,1)S(1)}, bf16[1,2048,512]{2,1,0:T(8,128)(2,1)}, u32[]{:S(2)}) copy-start(bf16[1,2048,512]{2,1,0:T(8,128)(2,1)} %param.22) | copy-start | bytes 6291460
  222.1 5.3 copy-start.25
  222.1 23.3 %all-to-all-start.4 = ((bf16[16,72,512]{2,1,0:T(8,128)(2,1)}), bf16[16,72,512]{2,1,0:T(8,128)(2,1)}, u32[]{:S(2)}, u32[]{:S(2)}) async-start(bf16[16,72,512]{2,1,0:T(8,128)(2,1)} %bitcast.34), calls=%async_computation.4 | async-start | bytes 2359296 | tf_op jit(solution)/shard_map/all_to_all | solution.py:200
  227.3 286.7 %all-reduce.11.cloned.1.call-start = ((), (), s32[]{:S(2)}) async-start(), calls=%async_computation.6 | async-start | bytes 8388608 | tf_op jit(solution)/shard_map/psum | solution.py:222
  231.3 6.2 %copy-start.24 = (bf16[1152,512]{1,0:T(8,128)(2,1)S(1)}, bf16[1152,512]{1,0:T(8,128)(2,1)}, u32[]{:S(2)}) copy-start(bf16[1152,512]{1,0:T(8,128)(2,1)} %fusion.27) | copy-start | bytes 3538948
  232.8 16.2 %collective-permute-start.2 = (bf16[6,48,512]{2,1,0:T(8,128)(2,1)S(1)}, bf16[6,48,512]{2,1,0:T(8,128)(2,1)S(1)}, u32[]{:S(2)}, u32[]{:S(2)}) collective-permute-start(bf16[6,48,512]{2,1,0:T(8,128)(2,1)S(1)} %bitcast.160), channel_id=1, source_target_pairs={{0,15},{1,0},{2,1},{3,2},{4,3},{5,4},{6,5},{7,6},{8,7},{9,8},{10,9... | collective-permute-start | bytes 884744 | tf_op jit(solution)/shard_map/ppermute | solution.py:17
  244.1 276.8 %all-reduce.9.cloned.1.call-start = ((), (), s32[]{:S(2)}) async-start(), calls=%async_computation.5 | async-start | bytes 8388608 | tf_op jit(solution)/shard_map/psum | solution.py:225
  257.3 8.8 %copy-start.29 = (bf16[4,144,1,16,32]{1,0,4,3,2:T(4,128)(2,1)S(1)}, bf16[4,144,1,16,32]{1,0,4,3,2:T(4,128)(2,1)}, u32[]{:S(2)}) copy-start(bf16[4,144,1,16,32]{1,0,4,3,2:T(4,128)(2,1)} %get-tuple-element.73) | copy-start | bytes 1769476
  266.0 7.1 %copy-start.28 = (bf16[4,144,1,16,32]{1,0,4,3,2:T(4,128)(2,1)S(1)}, bf16[4,144,1,16,32]{1,0,4,3,2:T(4,128)(2,1)}, u32[]{:S(2)}) copy-start(bf16[4,144,1,16,32]{1,0,4,3,2:T(4,128)(2,1)} %get-tuple-element.72) | copy-start | bytes 1769476
  266.0 15.7 %slice-start = ((s8[4718592]{0:T(1024)(128)(4,1)}), s8[4194304]{0:T(1024)(128)(4,1)S(1)}, s32[]{:S(2)}) async-start(s8[4718592]{0:T(1024)(128)(4,1)} %bitcast.135), calls=%async_computation.7 | async-start | bytes 8388608
  273.1 8.6 %slice-start.1 = ((s8[4718592]{0:T(1024)(128)(4,1)}), s8[524288]{0:T(1024)(128)(4,1)S(1)}, s32[]{:S(2)}) async-start(s8[4718592]{0:T(1024)(128)(4,1)} %bitcast.135), calls=%async_computation.8 | async-start | bytes 1048576
  273.2 8.6 %copy-start.11 = (bf16[4,144,16,32]{1,0,3,2:T(4,128)(2,1)S(1)}, bf16[4,144,16,32]{1,0,3,2:T(4,128)(2,1)}, u32[]{:S(2)}) copy-start(bf16[4,144,16,32]{1,0,3,2:T(4,128)(2,1)} %reshape_reshape.19) | copy-start | bytes 1769476
  291.5 6.5 %copy-start.7 = (f32[576,512]{1,0:T(8,128)S(1)}, f32[576,512]{1,0:T(8,128)}, u32[]{:S(2)}) copy-start(f32[576,512]{1,0:T(8,128)} %copy-done.6) | copy-start | bytes 3538948
  291.5 6.5 %copy-start.42 = (f32[576]{0:T(1024)S(1)}, f32[576]{0:T(1024)}, u32[]{:S(2)}) copy-start(f32[576]{0:T(1024)} %copy-done.41) | copy-start | bytes 6916
  309.6 203.5 %collective-permute-start.3 = (bf16[6,48,512]{2,1,0:T(8,128)(2,1)S(1)}, bf16[6,48,512]{2,1,0:T(8,128)(2,1)S(1)}, u32[]{:S(2)}, u32[]{:S(2)}) collective-permute-start(bf16[6,48,512]{2,1,0:T(8,128)(2,1)S(1)} %get-tuple-element.74), channel_id=1, source_target_pairs={{0,1},{1,2},{2,3},{3,4},{4,5},{5,6},{6,7},{7,8},{8,9},{9,10},{10,1... | collective-permute-start | bytes 884744 | tf_op jit(solution)/shard_map/ppermute | solution.py:17
  (33 other events, 71.2 us)
Sparse Core Ops, SparseCore 0:
  244.2 70.6 all-reduce.10
  320.6 156.4 all-reduce.8
where the time goes:
time: 541 us; the launch traced here: 533 us
  other arithmetic  158 us (29%)
  local copies, waits for them, and re-layouts  138 us (26%)
  matrix products  95.7 us (18%)
  blocking collectives  68.3 us (13%)
  starting transfers between devices  41.3 us (8%)
  waiting for transfers between devices  16.5 us (3%)
  between operations  15.4 us (3%)
    scatter-add x1, other arithmetic, core_attention(): rel_bias = jnp.take(table, relative_index(WINDOW), axis=1)  112 us
    psum x1, blocking collectives, on_device(): lax.psum((weight_grads[0], weight_grads[1], weight_grads[2], weight_grads...  68.3 us
    gather x2, local copies, waits for them, and re-layouts, core_attention(): rel_bias = jnp.take(table, relative_index(WINDOW), axis=1)  51 us
    unnamed x112, local copies, waits for them, and re-layouts  18.1 us
    dot_general x2, matrix products, core_attention(): jnp.einsum('nqhd,nkhd->nhqk', split_qkv[:, :, 0], split_qkv[:, :, 1], pre...  15.7 us
    ppermute x4, starting transfers between devices, shifted(): return lax.ppermute(value, axis, pairs)  11.3 us
    reduce_sum x1, local copies, waits for them, and re-layouts, core_attention(): logits = logits + rel_bias[None] + mask_add[:, None]  11.1 us
  transfers between devices with their start and end apart: 11, of which 4 were waited for; matrix products, arithmetic and copies ran while one was open for 67% of the time, Pallas kernels for 0%

commit v1 on v0

v1 whole, which is shorter than its diff:
```python
import functools

import jax
import jax.numpy as jnp
import numpy as np
from jax import lax
from jax.experimental import pallas as pl
from jax.experimental.pallas import tpu as pltpu
from jax.sharding import PartitionSpec as P

HEADS = 16
WINDOW = 12
SHIFT = 6
TOKENS = WINDOW * WINDOW
HALF = TOKENS // 2
SIDE = 2 * WINDOW - 1
SPAN = 384
TABLE_PAD = 640
SCALE = 32**-0.5
EXPERT_ROWS = 384
TAIL = (
    0.0997355664,
    0.0997364567,
    0.0934658327,
    0.0816079977,
    0.0589507659,
    0.0637694228,
    -0.0318383035,
    0.0957188375,
    -0.0809437035,
    0.0197971106,
)
VMEM_LIMIT = 40 * 1024 * 1024
ATTEND_LIMIT = 60 * 1024 * 1024
F32 = jnp.float32
BF16 = jnp.bfloat16
GROUP = ("x", "core")
SAME_CORE = ("x", "tile")
OWNERS = 64


def nn(a, b):
    return lax.dot_general(a, b, (((1,), (0,)), ((), ())), preferred_element_type=F32)


def nt(a, b):
    return lax.dot_general(a, b, (((1,), (1,)), ((), ())), preferred_element_type=F32)


def tn(a, b):
    return lax.dot_general(a, b, (((0,), (0,)), ((), ())), preferred_element_type=F32)


def call(kernel, outs, *, grid=None, in_specs=None, out_specs=None, scratch=(), cost=None, limit=VMEM_LIMIT):
    extra = {}
    if grid is not None:
        extra = dict(grid=grid, in_specs=in_specs, out_specs=out_specs)
    if cost is not None:
        extra["cost_estimate"] = pl.CostEstimate(flops=cost[0], bytes_accessed=cost[1], transcendentals=cost[2])
    return pl.pallas_call(
        kernel,
        out_shape=outs,
        scratch_shapes=list(scratch),
        compiler_params=pltpu.CompilerParams(vmem_limit_bytes=limit),
        **extra,
    )


def shape(dims, dtype):
    return jax.ShapeDtypeStruct(dims, dtype)


def whole(*dims):
    return pl.BlockSpec(dims, lambda *_: (0,) * len(dims))


def shifted(value, axis, steps):
    count = lax.axis_size(axis)
    pairs = [(source, (source + steps) % count) for source in range(count)]
    return lax.ppermute(value, axis, pairs)


def half_order(col_windows):
    columns = col_windows * WINDOW
    pick = np.zeros((SHIFT * columns, SHIFT * columns), np.float32)
    for win in range(col_windows):
        for row in range(SHIFT):
            for col in range(WINDOW):
                source = row * columns + (win * WINDOW + SHIFT + col) % columns
                pick[win * HALF + row * WINDOW + col, source] = 1.0
    return pick


def bias_targets():
    lane = np.arange(SPAN)
    target = (lane // WINDOW) * SIDE + lane % WINDOW + WINDOW - 1
    return np.where(lane < SIDE * WINDOW, target, -1000).astype(np.int32)[None]


def window_masks(row_last, col_windows):
    inner_pos = jnp.arange(TOKENS, dtype=jnp.int32)
    row_in = inner_pos // WINDOW
    col_in = inner_pos % WINDOW
    row_region = jnp.where(row_last[:, None], jnp.where(row_in < SHIFT, 1, 2)[None], 0)
    col_last = jnp.arange(col_windows, dtype=jnp.int32) == col_windows - 1
    col_region = jnp.where(col_last[:, None], jnp.where(col_in < SHIFT, 1, 2)[None], 0)
    region = (row_region[:, None, :] * 3 + col_region[None, :, :]).reshape(-1, TOKENS)
    same = region[:, :, None] == region[:, None, :]
    return jnp.where(same, 0.0, -100.0).astype(F32)


def normalised(values):
    mean = jnp.mean(values, axis=-1, keepdims=True)
    centred = values - mean
    scale = lax.rsqrt(jnp.mean(centred * centred, axis=-1, keepdims=True) + 1e-05)
    return centred * scale, scale


def norm_backward(unit, scale, grad, gain):
    weighted = grad * gain
    along = jnp.mean(weighted * unit, axis=-1, keepdims=True)
    flat = jnp.mean(weighted, axis=-1, keepdims=True)
    return scale * (weighted - flat - unit * along), jnp.sum(grad * unit, axis=0, keepdims=True)


def normal_of(values):
    bell = jnp.exp(-0.5 * values * values)
    inverse = 1.0 / (1.0 + 0.25 * jnp.abs(values))
    ratio = jnp.full_like(values, TAIL[-1])
    for factor in TAIL[-2::-1]:
        ratio = ratio * inverse + factor
    tail = bell * (ratio * inverse)
    return jnp.where(values < 0.0, tail, 1.0 - tail), bell * 0.3989422804014327


def iota(dims, axis):
    return lax.broadcasted_iota(jnp.int32, dims, axis)


def spread_matrix(targets, col):
    hit = iota((TABLE_PAD, SPAN), 0) == targets - col
    return jnp.where(hit, 1.0, 0.0).astype(BF16)


def pieces_of(value, count):
    parts = []
    for _ in range(count):
        part = value.astype(BF16)
        parts.append(part)
        value = value - part.astype(F32)
    return parts


def route_kernel(capacity, routes_ref, gate_ref, grad_ref, order_ref, send_ref, row_ref, col_ref):
    rows = grad_ref.shape[0]
    slots = send_ref.shape[0]
    routes = routes_ref[...]
    chosen = jnp.where(iota((HEADS, rows), 0) == routes, 1.0, 0.0)
    upto = jnp.where(iota((rows, rows), 0) <= iota((rows, rows), 1), 1.0, 0.0).astype(BF16)
    running = nn(chosen.astype(BF16), upto)
    slot = jnp.sum(running * chosen, axis=0, keepdims=True) - 1.0
    expert = routes.astype(F32)
    place = (expert * capacity + slot).astype(jnp.int32)
    picks = jnp.where(iota((slots, rows), 0) == place, gate_ref[...].astype(F32), 0.0).astype(BF16)
    send_ref[...] = nn(picks, grad_ref[...]).astype(BF16)
    order = order_ref[...]
    both = jnp.concatenate(
        [jnp.broadcast_to(expert, (8, rows)), jnp.broadcast_to(slot, (8, rows))], axis=0
    ).astype(BF16)
    moved = nt(both, order)
    there = moved[0:1] * capacity + moved[8:9]
    row_ref[...] = there.astype(jnp.int32)
    same = iota((rows, rows), 0) == iota((rows, rows), 1)
    col_ref[...] = jnp.sum(jnp.where(same, there, 0.0), axis=1, keepdims=True).astype(jnp.int32)


def bias_kernel(table_ref, targets_ref, bias_ref, spread):
    table = jnp.concatenate(pieces_of(table_ref[...], 3), axis=0)
    for col in range(16):
        part = nn(table, spread_matrix(targets_ref[...], col % WINDOW))
        spread[col] = part[0:HEADS] + part[HEADS : 2 * HEADS] + part[2 * HEADS :]
    for head in range(HEADS):
        rows = spread[:, head, :]
        for row in range(WINDOW):
            start = (WINDOW - 1 - row) * WINDOW
            turned = pltpu.roll(rows, (SPAN - start) % SPAN, 1) if start else rows
            bias_ref[head, row * WINDOW : (row + 1) * WINDOW, :] = turned[:WINDOW, :TOKENS]


def table_kernel(pair_ref, targets_ref, gain_one_ref, gain_two_ref, out_ref, wide, lined):
    wide[...] = jnp.zeros_like(wide)
    for head in range(HEADS):
        wide[:TOKENS, :TOKENS] = pair_ref[head]
        total = wide[(WINDOW - 1) * WINDOW : (WINDOW - 1) * WINDOW + 16, :]
        for row in range(WINDOW - 1):
            start = (WINDOW - 1 - row) * WINDOW
            total = total + pltpu.roll(wide[row * WINDOW : row * WINDOW + 16, :], start, 1)
        lined[head] = total
    grads = jnp.zeros((2 * HEADS, TABLE_PAD), F32)
    for col in range(WINDOW):
        value = jnp.concatenate(pieces_of(lined[:, col, :], 2), axis=0)
        grads = grads + nt(value, spread_matrix(targets_ref[...], col))
    grads = grads[:HEADS] + grads[HEADS:]
    out_ref[...] = jnp.zeros_like(out_ref)
    lines = [grads[head : head + 1, 128 * part : 128 * part + 128] for head in range(HEADS) for part in range(5)]
    for gain_ref in (gain_one_ref, gain_two_ref):
        lines += [gain_ref[:, 128 * part : 128 * part + 128] for part in range(4)]
    for number, line in enumerate(lines):
        high, low = pieces_of(line, 2)
        out_ref[number // 2, number % 2 : number % 2 + 1, :] = high.astype(F32)
        out_ref[number // 2, 2 + number % 2 : 3 + number % 2, :] = low.astype(F32)


def merge_kernel(mine_ref, other_ref, small_ref, out_ref):
    for owner in range(OWNERS):
        both = mine_ref[owner].astype(F32) + other_ref[owner].astype(F32)
        out_ref[owner, :, :512] = both.astype(BF16)
        out_ref[owner, :, 512:] = small_ref[owner].astype(BF16)


def sum_kernel(all_ref, out_ref):
    total = all_ref[0].astype(F32)
    for owner in range(1, OWNERS):
        total = total + all_ref[owner].astype(F32)
    small = total[:, 512:]
    small = small + pltpu.roll(small, 14, 0)
    high = small.astype(BF16).astype(F32)
    low = pltpu.roll(small - high, 2, 0)
    row = iota(small.shape, 0)
    small = jnp.where(row < 2, high, jnp.where(row < 4, low, 0.0))
    total = jnp.concatenate([total[:, :512], small], axis=1).astype(BF16)
    for owner in range(OWNERS):
        out_ref[owner] = total


def unpack_kernel(core_ref, mine_ref, other_ref, qkv_ref, proj_ref, small_ref):
    def place(half_ref, first):
        for row in range(16):
            here = slice(first + 16 * row, first + 16 * row + 16)
            for col in range(4):
                block = half_ref[4 * row + col].astype(F32)
                qkv_ref[here, 384 * col : 384 * col + 384] = block[:, :384]
                proj_ref[here, 128 * col : 128 * col + 128] = block[:, 384:512]

    @pl.when(core_ref[0] == 0)
    def _():
        place(mine_ref, 0)
        place(other_ref, 256)

    @pl.when(core_ref[0] != 0)
    def _():
        place(other_ref, 0)
        place(mine_ref, 256)

    for owner in range(OWNERS):
        small = mine_ref[owner, :, 512:].astype(F32) + other_ref[owner, :, 512:].astype(F32)
        small_ref[owner] = small + pltpu.roll(small, 14, 0)


def attend_kernel(
    image_ref, below_ref, order_ref, gain_ref, w_qkv_ref, w_proj_ref, bias_ref, mask_ref,
    prob_ref, qkv_ref, x_ref, normed_ref, mixed_ref, own_ref, send_ref, blended,
):
    group = pl.program_id(0)
    wins = x_ref.shape[0] // TOKENS
    lanes = iota((TOKENS, 128), 1) // 32

    @pl.when(group == 0)
    def _():
        order = order_ref[...]
        upper = nn(order, image_ref[...])
        lower = nn(order, below_ref[...])
        parts = []
        for win in range(wins):
            parts.append(upper[win * HALF : (win + 1) * HALF])
            parts.append(lower[win * HALF : (win + 1) * HALF])
        x = jnp.concatenate(parts, axis=0)
        x_ref[...] = x.astype(BF16)
        unit, _ = normalised(x)
        normed_ref[...] = (unit * gain_ref[...]).astype(BF16)
        normed = normed_ref[...]
        for pair in range(6):
            act = nn(normed, w_qkv_ref[:, 256 * pair : 256 * pair + 256]).astype(BF16)
            qkv_ref[2 * pair] = act[:, :128]
            qkv_ref[2 * pair + 1] = act[:, 128:]

    for win in range(wins):
        rows = slice(win * TOKENS, (win + 1) * TOKENS)
        query = qkv_ref[group, rows, :]
        key = qkv_ref[4 + group, rows, :]
        value_t = jnp.transpose(qkv_ref[8 + group, rows, :].astype(F32)).astype(BF16)
        mask = mask_ref[int(win == wins - 1)]
        mixes = []
        for head in range(4):
            own = jnp.where(lanes == head, query, jnp.zeros_like(query))
            score = nt(key, own) * SCALE + bias_ref[head] + mask
            score = jnp.exp(score - jnp.max(score, axis=0, keepdims=True))
            prob = (score * (1.0 / jnp.sum(score, axis=0, keepdims=True))).astype(BF16)
            prob_ref[head, win] = prob
            mixes.append(nn(value_t[32 * head : 32 * head + 32], prob))
        mix = jnp.transpose(jnp.concatenate(mixes, axis=0))
        blended[group, rows, :] = mix.astype(BF16)

    @pl.when(group == pl.num_programs(0) - 1)
    def _():
        mixed = jnp.concatenate([blended[i] for i in range(4)], axis=1)
        mixed_ref[...] = mixed
        after = x_ref[...].astype(F32) + nn(mixed, w_proj_ref[...])
        kept = [after[win * TOKENS : win * TOKENS + HALF] for win in range(wins)]
        away = [after[win * TOKENS + HALF : (win + 1) * TOKENS] for win in range(wins)]
        own_ref[...] = jnp.concatenate(kept, axis=0)
        send_ref[...] = jnp.concatenate(away, axis=0).astype(BF16)


def dispatch_kernel(own_ref, above_ref, gain_ref, row_ref, send_ref, after_ref):
    after = jnp.concatenate([above_ref[...].astype(F32), own_ref[...]], axis=0)
    after_ref[...] = after
    unit, _ = normalised(after)
    normed = (unit * gain_ref[...]).astype(BF16)
    picks = iota((send_ref.shape[0], after.shape[0]), 0) == row_ref[...]
    send_ref[...] = nn(jnp.where(picks, 1.0, 0.0).astype(BF16), normed).astype(BF16)


def expert_kernel(in_ref, back_ref, w_up_ref, hidden_ref, pre_ref, out_ref, total, score):
    step = pl.program_id(0)
    rows = in_ref.shape[0]
    width = out_ref.shape[1] - 128

    @pl.when(step == 0)
    def _():
        total[...] = jnp.zeros_like(total)
        score[...] = jnp.zeros_like(score)

    w_up = w_up_ref[...]
    for block in range(rows // EXPERT_ROWS):
        here = slice(block * EXPERT_ROWS, (block + 1) * EXPERT_ROWS)
        pre = nn(in_ref[here, :], w_up)
        cumulative, density = normal_of(pre)
        hidden = (pre * cumulative).astype(BF16)
        back = back_ref[here, :].astype(F32)
        grad = (back * (cumulative + pre * density)).astype(BF16)
        hidden_ref[here, :] = hidden
        pre_ref[here, :] = grad
        product = hidden.astype(F32) * back
        score[here, :] += product[:, :128] + product[:, 128:]
        total[here, :] += nt(grad, w_up)

    @pl.when(step == pl.num_programs(0) - 1)
    def _():
        out_ref[:, :width] = total[...].astype(BF16)
        summed = jnp.sum(score[...], axis=1, keepdims=True)
        high = summed.astype(BF16).astype(F32)
        lane = iota((rows, 128), 1)
        tail = jnp.where(lane == 0, high, jnp.where(lane == 1, summed - high, 0.0))
        out_ref[:, width:] = tail.astype(BF16)


def combine_kernel(
    back_ref, col_ref, after_ref, grad_ref, order_ref, gain_ref, send_ref, own_ref, gain_out_ref, score_ref
):
    rows, width = after_ref.shape
    picks = iota((rows, back_ref.shape[0]), 1) == col_ref[...]
    picks = jnp.where(picks, 1.0, 0.0).astype(BF16)
    back = nn(picks, back_ref[...])
    score_ref[...] = back[:, width:]
    unit, scale = normalised(after_ref[...])
    grad, gain_grad = norm_backward(unit, scale, back[:, :width], gain_ref[...])
    gain_out_ref[...] = gain_grad
    order = order_ref[...]
    half = rows // 2
    send_ref[...] = (nn(order, grad_ref[:half, :]) + grad[:half]).astype(BF16)
    own_ref[...] = nn(order, grad_ref[half:, :]) + grad[half:]


def attend_backward_kernel(
    core_ref, own_ref, below_ref, order_t_ref, gain_ref, w_qkv_ref, w_proj_ref, qkv_ref, x_ref, normed_ref, mixed_ref,
    prob_ref, pair_ref, mine_ref, other_ref, kept_ref, send_ref, gain_out_ref, cotangent, grad_mixed, grad_act,
    grad_qkv, grad_proj,
):
    group = pl.program_id(0)
    rows_all = x_ref.shape[0]
    wins = rows_all // TOKENS
    lanes = iota((TOKENS, 128), 1) // 32

    @pl.when(group == 0)
    def _():
        parts = []
        for win in range(wins):
            parts.append(own_ref[win * HALF : (win + 1) * HALF, :])
            parts.append(below_ref[...].astype(F32)[win * HALF : (win + 1) * HALF, :])
        cot = jnp.concatenate(parts, axis=0)
        cotangent[...] = cot
        mixed = nt(cot.astype(BF16), w_proj_ref[...]).astype(BF16)
        for i in range(4):
            grad_mixed[i] = mixed[:, 128 * i : 128 * i + 128]

    pair_ref[...] = jnp.zeros_like(pair_ref)

    for win in range(wins):
        rows = slice(win * TOKENS, (win + 1) * TOKENS)
        query = qkv_ref[group, rows, :]
        key = qkv_ref[4 + group, rows, :]
        value = qkv_ref[8 + group, rows, :]
        out = grad_mixed[group, rows, :]
        key_t = jnp.transpose(key.astype(F32)).astype(BF16)
        grad_query, grad_key, grad_value = [], None, None
        for head in range(4):
            own_out = jnp.where(lanes == head, out, jnp.zeros_like(out))
            own_query = jnp.where(lanes == head, query, jnp.zeros_like(query))
            half_prob = prob_ref[head, win]
            prob = half_prob.astype(F32)
            grad_prob = nt(value, own_out).astype(BF16).astype(F32)
            weighted = prob * grad_prob
            grad_score = weighted - prob * jnp.sum(weighted, axis=0, keepdims=True)
            pair_ref[head] += grad_score
            half_score = grad_score.astype(BF16)
            part_value = nn(half_prob, own_out)
            part_key = nn(half_score, own_query)
            grad_value = part_value if head == 0 else grad_value + part_value
            grad_key = part_key if head == 0 else grad_key + part_key
            grad_query.append(nn(key_t[32 * head : 32 * head + 32], half_score))
        full_query = jnp.transpose(jnp.concatenate(grad_query, axis=0))
        grad_act[group, rows, :] = (full_query * SCALE).astype(BF16)
        grad_act[4 + group, rows, :] = (grad_key * SCALE).astype(BF16)
        grad_act[8 + group, rows, :] = grad_value.astype(BF16)

    @pl.when(group == pl.num_programs(0) - 1)
    def _():
        act = jnp.concatenate([grad_act[i] for i in range(12)], axis=1)
        normed_t = jnp.transpose(normed_ref[...].astype(F32)).astype(BF16)
        mixed_t = jnp.transpose(mixed_ref[...].astype(F32)).astype(BF16)
        cot = cotangent[...]
        grad_proj[...] = nn(mixed_t, cot.astype(BF16)).astype(BF16)
        grad_qkv[...] = nn(normed_t, act).astype(BF16)

        def scatter(half_ref, first):
            for row in range(16):
                here = slice(first + 16 * row, first + 16 * row + 16)
                for col in range(4):
                    half_ref[4 * row + col, :, :384] = grad_qkv[here, 384 * col : 384 * col + 384]
                    half_ref[4 * row + col, :, 384:] = grad_proj[here, 128 * col : 128 * col + 128]

        @pl.when(core_ref[0] == 0)
        def _():
            scatter(mine_ref, 0)
            scatter(other_ref, 256)

        @pl.when(core_ref[0] != 0)
        def _():
            scatter(other_ref, 0)
            scatter(mine_ref, 256)

        grad_normed = nt(act, w_qkv_ref[...])
        unit, scale = normalised(x_ref[...].astype(F32))
        grad, gain_grad = norm_backward(unit, scale, grad_normed, gain_ref[...])
        gain_out_ref[...] = gain_grad
        total = cot + grad
        kept = [total[win * TOKENS : win * TOKENS + HALF] for win in range(wins)]
        away = [total[win * TOKENS + HALF : (win + 1) * TOKENS] for win in range(wins)]
        order_t = order_t_ref[...]
        kept_ref[...] = nn(order_t, jnp.concatenate(kept, axis=0).astype(BF16)).astype(BF16)
        send_ref[...] = nn(order_t, jnp.concatenate(away, axis=0).astype(BF16)).astype(BF16)


def on_device(
    image, grad_out, gate, routes, gain_one, w_qkv, w_proj, table, gain_two, w_fc1, w_fc2
):
    tile_count = lax.axis_size("tile")
    tile_index = lax.axis_index("tile")
    strip_height, columns, channels = image.shape[1:]
    wins = columns // WINDOW
    rows = strip_height * columns
    half = rows // 2
    capacity = 2 * rows // tile_count
    slots = tile_count * capacity
    ffn = w_fc1.shape[2]
    core = lax.axis_index("core").reshape(1).astype(jnp.int32)
    exchange = functools.partial(lax.all_to_all, split_axis=0, concat_axis=0, tiled=True)
    pick = half_order(wins)
    order = jnp.asarray(pick, BF16)
    order_t = jnp.asarray(pick.T, BF16)
    order_all = jnp.asarray(np.kron(np.eye(2), pick), BF16)
    targets = jnp.asarray(bias_targets())
    gain_one = gain_one.reshape(1, channels)
    gain_two = gain_two.reshape(1, channels)
    image_rows = image.reshape(rows, channels)
    grad_rows = grad_out.reshape(rows, channels)
    gate_row = gate.reshape(1, rows)

    below = shifted(image_rows[:half], "tile", -1)
    send_grad, place_row, place_col = call(
        functools.partial(route_kernel, capacity),
        (shape((slots, channels), BF16), shape((1, rows), jnp.int32), shape((rows, 1), jnp.int32)),
        cost=(700000000, 3000000, 0),
    )(routes.reshape(1, rows), gate_row, grad_rows, order_all)
    recv_grad = exchange(send_grad, "tile")
    bias = call(
        bias_kernel,
        shape((HEADS, TOKENS, TOKENS), F32),
        scratch=[pltpu.VMEM((16, HEADS, SPAN), F32)],
        cost=(400000000, 3000000, 0),
    )(jnp.pad(table, ((0, 0), (0, TABLE_PAD - table.shape[1]))), targets)
    mask = window_masks(jnp.reshape(tile_index == tile_count - 1, (1,)), wins)[wins - 2 :]

    head_block = pl.BlockSpec((4, wins, TOKENS, TOKENS), lambda g: (g, 0, 0, 0))
    pair_block = pl.BlockSpec((4, TOKENS, TOKENS), lambda g: (g, 0, 0))
    prob, qkv_act, windows, normed_one, mixed, own_after, send_after = call(
        attend_kernel,
        (
            shape((HEADS, wins, TOKENS, TOKENS), BF16),
            shape((12, rows, 128), BF16),
            shape((rows, channels), BF16),
            shape((rows, channels), BF16),
            shape((rows, channels), BF16),
            shape((half, channels), F32),
            shape((half, channels), BF16),
        ),
        grid=(4,),
        in_specs=[
            pl.BlockSpec((half, channels), lambda g: (1, 0)),
            whole(half, channels),
            whole(half, half),
            whole(1, channels),
            whole(channels, 3 * channels),
            whole(channels, channels),
            pair_block,
            whole(2, TOKENS, TOKENS),
        ],
        out_specs=(
            head_block,
            whole(12, rows, 128),
            whole(rows, channels),
            whole(rows, channels),
            whole(rows, channels),
            whole(half, channels),
            whole(half, channels),
        ),
        scratch=[pltpu.VMEM((4, rows, 128), BF16)],
        cost=(3000000000, 12000000, 2000000),
        limit=ATTEND_LIMIT,
    )(image_rows, below, order, gain_one, w_qkv, w_proj, bias, mask)

    above = shifted(send_after, "tile", 1)
    send_in, after = call(
        dispatch_kernel,
        (shape((slots, channels), BF16), shape((rows, channels), F32)),
        cost=(700000000, 4000000, 0),
    )(own_after, above, gain_two, place_row)
    recv_in = exchange(send_in, "tile")

    w_up, w_down = w_fc1[0], w_fc2[0]
    grad_hidden = jnp.dot(recv_grad, w_down.T, preferred_element_type=F32).astype(BF16)
    chunk = 256
    strip = pl.BlockSpec((slots, chunk), lambda f: (0, f))
    hidden, grad_pre, send_back = call(
        expert_kernel,
        (
            shape((slots, ffn), BF16),
            shape((slots, ffn), BF16),
            shape((slots, channels + 128), BF16),
        ),
        grid=(ffn // chunk,),
        in_specs=[whole(slots, channels), strip, pl.BlockSpec((channels, chunk), lambda f: (0, f))],
        out_specs=(strip, strip, whole(slots, channels + 128)),
        scratch=[pltpu.VMEM((slots, channels), F32), pltpu.VMEM((slots, 128), F32)],
        cost=(4800000000, 20000000, 5000000),
    )(recv_in, grad_hidden, w_up)
    recv_back = exchange(send_back, "tile")
    grad_up = jnp.dot(recv_in.T, grad_pre, preferred_element_type=F32).astype(BF16)
    grad_down = jnp.dot(hidden.T, recv_grad, preferred_element_type=F32).astype(BF16)
    recv_back, grad_up, grad_down = lax.optimization_barrier((recv_back, grad_up, grad_down))
    summed_up, summed_down = lax.psum((grad_up, grad_down), GROUP)

    send_cot, own_cot, gain_two_part, score = call(
        combine_kernel,
        (
            shape((half, channels), BF16),
            shape((half, channels), F32),
            shape((1, channels), F32),
            shape((rows, 128), F32),
        ),
        cost=(1000000000, 7000000, 0),
    )(recv_back, place_col, after, grad_rows, order, gain_two)
    below_cot = shifted(send_cot, "tile", -1)
    score = (score[:, 0] + score[:, 1]).reshape(2, wins, SHIFT, WINDOW)
    score = score.transpose(0, 2, 1, 3).reshape(strip_height, columns)
    grad_gate = jnp.roll(score, SHIFT, axis=1) / gate[0].astype(F32)

    half_pieces = shape((OWNERS, 16, 512), BF16)
    pair, mine, other, kept, send_up, gain_one_part = call(
        attend_backward_kernel,
        (
            shape((HEADS, TOKENS, TOKENS), F32),
            half_pieces,
            half_pieces,
            shape((half, channels), BF16),
            shape((half, channels), BF16),
            shape((1, channels), F32),
        ),
        grid=(4,),
        in_specs=[
            pl.BlockSpec(memory_space=pltpu.SMEM),
            whole(half, channels),
            whole(half, channels),
            whole(half, half),
            whole(1, channels),
            whole(channels, 3 * channels),
            whole(channels, channels),
            whole(12, rows, 128),
            whole(rows, channels),
            whole(rows, channels),
            whole(rows, channels),
            head_block,
        ],
        out_specs=(
            pair_block,
            whole(OWNERS, 16, 512),
            whole(OWNERS, 16, 512),
            whole(half, channels),
            whole(half, channels),
            whole(1, channels),
        ),
        scratch=[
            pltpu.VMEM((rows, channels), F32),
            pltpu.VMEM((4, rows, 128), BF16),
            pltpu.VMEM((12, rows, 128), BF16),
            pltpu.VMEM((channels, 3 * channels), BF16),
            pltpu.VMEM((channels, channels), BF16),
        ],
        cost=(6000000000, 18000000, 0),
        limit=ATTEND_LIMIT,
    )(core, own_cot, below_cot, order_t, gain_one, w_qkv, w_proj, qkv_act, windows, normed_one, mixed, prob)
    upper = shifted(send_up, "tile", 1)
    other = shifted(other, "core", 1)
    small = call(
        table_kernel,
        shape((OWNERS, 16, 128), F32),
        scratch=[pltpu.VMEM((TOKENS + 16, SPAN), F32), pltpu.VMEM((HEADS, 16, SPAN), F32)],
        cost=(400000000, 3000000, 0),
    )(pair, targets, gain_one_part, gain_two_part)
    pieces = shape((OWNERS, 16, 640), BF16)
    merged = call(merge_kernel, pieces, cost=(0, 4000000, 0))(mine, other, small)
    parts = exchange(merged, SAME_CORE)
    parts, upper = lax.optimization_barrier((parts, upper))
    summed = call(sum_kernel, pieces, cost=(0, 4000000, 0))(parts)
    grad_image = jnp.concatenate([upper, kept], axis=0).reshape(image.shape)
    gathered = exchange(summed, SAME_CORE)
    grad_qkv, grad_proj, small_all = call(
        unpack_kernel,
        (
            shape((channels, 3 * channels), F32),
            shape((channels, channels), F32),
            shape((OWNERS, 16, 128), F32),
        ),
        grid=(1,),
        in_specs=[pl.BlockSpec(memory_space=pltpu.SMEM), whole(OWNERS, 16, 640), whole(OWNERS, 16, 640)],
        out_specs=(whole(channels, 3 * channels), whole(channels, channels), whole(OWNERS, 16, 128)),
        cost=(0, 7000000, 0),
    )(core, gathered, shifted(gathered, "core", 1))
    small_all = small_all[:, :2, :].reshape(2 * OWNERS, 128)
    first = HEADS * TABLE_PAD // 128
    grad_table = small_all[:first].reshape(HEADS, TABLE_PAD)[:, : table.shape[1]]
    grad_gain_one = small_all[first : first + 4].reshape(channels)
    grad_gain_two = small_all[first + 4 : first + 8].reshape(channels)
    return (
        grad_image,
        grad_gate.reshape(1, strip_height, columns),
        summed_up.astype(F32).reshape(1, channels, ffn),
        summed_down.astype(F32).reshape(1, ffn, channels),
        grad_qkv,
        grad_proj,
        grad_table,
        grad_gain_one,
        grad_gain_two,
    )


def solution(mesh):
    devices = mesh.devices
    split = jax.sharding.Mesh(devices.reshape(-1, 2, devices.shape[1]), ("x", "core", "tile"))
    return jax.shard_map(
        on_device,
        mesh=split,
        in_specs=(
            P(GROUP, "tile", None, None),
            P(GROUP, "tile", None, None),
            P(GROUP, "tile", None),
            P(GROUP, "tile", None, None),
            P(),
            P(),
            P(),
            P(),
            P(),
            P("tile", None, None),
            P("tile", None, None),
        ),
        out_specs=(
            P(GROUP, "tile", None, None),
            P(GROUP, "tile", None),
            P("tile", None, None),
            P("tile", None, None),
            P(),
            P(),
            P(),
            P(),
            P(),
        ),
        check_vma=False,
    )
```

time: 541 us -> 328 us (0.61); the launches traced: 533 us -> 326 us
  other arithmetic: 158 us -> 9.72 us
  local copies, waits for them, and re-layouts: 138 us -> 22.8 us
  waiting for transfers between devices: 16.5 us -> 128 us
  Pallas kernels: 0 us -> 84 us
  matrix products: 95.7 us -> 18.2 us
  blocking collectives: 68.3 us -> 0 us
  starting transfers between devices: 41.3 us -> 48.4 us
    scatter-add x1 -> x0, other arithmetic: 112 us -> none  [core_attention(): rel_bias = jnp.take(table, relative_index(WINDOW), axis=1)]
    pallas_call x0 -> x11, Pallas kernels: none -> 84 us  [the longest x1 23.9 us: on_device(): call(attend_backward_kernel, (shape((HEADS, TOKENS, TOKENS), F32), half_p...]
    psum x1 -> x0, blocking collectives: 68.3 us -> none  [on_device(): lax.psum((weight_grads[0], weight_grads[1], weight_grads[2], weight_grads...]
    dot_general x23 -> x3, matrix products: 85.8 us -> 18.2 us  [the longest x1 7.08 us: on_device(): jnp.dot(recv_in.T, grad_pre, preferred_element_type=F32).astype(BF16)]
    psum x2 -> x1, waiting for transfers between devices: 0.01 us -> 53.3 us  [on_device(): summed_up, summed_down = lax.psum((grad_up, grad_down), GROUP)]
    gather x2 -> x0, local copies, waits for them, and re-layouts: 51 us -> none  [core_attention(): rel_bias = jnp.take(table, relative_index(WINDOW), axis=1)]
    ppermute x4 -> x6, waiting for transfers between devices: 0.51 us -> 38.7 us  [shifted(): return lax.ppermute(value, axis, pairs)]
    all_to_all x5, waiting for transfers between devices: 15.9 us -> 35.8 us  [the longest x1 18.7 us: on_device(): gathered = exchange(summed, SAME_CORE)]
  transfers between devices with their start and end apart: 11 -> 12, of which waited for: 4 -> 7; matrix products, arithmetic and copies ran while one was open for 67% -> 9% of each run, Pallas kernels for 0% -> 9%
where the time goes in v1:
time: 328 us; the launch traced here: 326 us
  waiting for transfers between devices  128 us (39%)
  Pallas kernels  84 us (26%)
  starting transfers between devices  48.4 us (15%)
  local copies, waits for them, and re-layouts  22.8 us (7%)
  matrix products  18.2 us (6%)
  between operations  14.3 us (4%)
  other arithmetic  9.72 us (3%)
    psum x1, waiting for transfers between devices, on_device(): summed_up, summed_down = lax.psum((grad_up, grad_down), GROUP)  53.3 us
    ppermute x6, waiting for transfers between devices, shifted(): return lax.ppermute(value, axis, pairs)  38.7 us
    pallas_call x1, Pallas kernels, on_device(): call(attend_backward_kernel, (shape((HEADS, TOKENS, TOKENS), F32), half_p...  23.9 us
    pallas_call x1, Pallas kernels, on_device(): call(expert_kernel, (shape((slots, ffn), BF16), shape((slots, ffn), BF16)...  22.6 us
    unnamed x65, local copies, waits for them, and re-layouts  19.3 us
    pallas_call x1, Pallas kernels, on_device(): call(attend_kernel, (shape((HEADS, wins, TOKENS, TOKENS), BF16), shape((1...  18.8 us
    ppermute x6, starting transfers between devices, shifted(): return lax.ppermute(value, axis, pairs)  18.7 us
    all_to_all x1, waiting for transfers between devices, on_device(): gathered = exchange(summed, SAME_CORE)  18.7 us
  transfers between devices with their start and end apart: 12, of which 7 were waited for; matrix products, arithmetic and copies ran while one was open for 9% of the time, Pallas kernels for 9%

profile of v1, /device:TPU:1, one launch (start us, length us, event | category | flops | bytes accessed | tf_op | source)
XLA Modules:
  0.0 325.9 jit_solution(12869628639871674937)
XLA Ops:
  8.3 7.1 %collective-permute-start = (bf16[288,512]{1,0:T(8,128)(2,1)S(1)}, bf16[288,512]{1,0:T(8,128)(2,1)S(1)}, u32[]{:S(2)}, u32[]{:S(2)}) collective-permute-start(bf16[288,512]{1,0:T(8,128)(2,1)S(1)} %bitcast.42), channel_id=1, source_target_pairs={{0,15},{1,0},{2,1},{3,2},{4,3},{5,4},{6,5},{7,6},{8,7},{9,8},{10,9... | collective-permute-start | bytes 884744 | tf_op jit(solution)/shard_map/ppermute | solution.py:80
  19.2 2.3 shard_map.216
  22.2 4.4 %all-to-all-start.1 = ((bf16[16,72,512]{2,1,0:T(8,128)(2,1)}), bf16[16,72,512]{2,1,0:T(8,128)(2,1)}, u32[]{:S(2)}, u32[]{:S(2)}) async-start(bf16[16,72,512]{2,1,0:T(8,128)(2,1)} %bitcast.8), calls=%async_computation.1 | async-start | bytes 2359296 | tf_op jit(solution)/shard_map/all_to_all | solution.py:496
  26.7 2.7 shard_map.214.bias_ref
  32.4 18.8 %shard_map.215 = (bf16[16,4,144,144]{3,2,1,0:T(8,128)(2,1)}, bf16[12,576,128]{2,1,0:T(8,128)(2,1)}, bf16[576,512]{1,0:T(8,128)(2,1)}, bf16[576,512]{1,0:T(8,128)...) custom-call(bf16[576,512]{1,0:T(8,128)(2,1)} %bitcast.43, ...), custom_call_target="tpu_custom_call" | custom-call | flops 3000000000 | bytes 12000000 | tf_op jit(solution)/shard_map/pallas_call | solution.py:507
  52.4 9.9 %collective-permute-done.1.above_ref = bf16[288,512]{1,0:T(8,128)(2,1)S(1)} collective-permute-done((bf16[288,512]{1,0:T(8,128)(2,1)}, bf16[288,512]{1,0:T(8,128)(2,1)S(1)}, u32[]{:S(2)}, u32[]{:S(2)}) %collective-permute-start.1) | collective-permute-done | bytes 294944 | tf_op jit(solution)/shard_map/ppermute | solution.py:80
  65.8 4.6 %all-to-all-start = ((bf16[16,72,512]{2,1,0:T(8,128)(2,1)}), bf16[16,72,512]{2,1,0:T(8,128)(2,1)}, u32[]{:S(2)}, u32[]{:S(2)}) async-start(bf16[16,72,512]{2,1,0:T(8,128)(2,1)} %bitcast.33), calls=%async_computation | async-start | bytes 2359296 | tf_op jit(solution)/shard_map/all_to_all | solution.py:549
  70.4 5.6 %convolution_convert_fusion.back_ref = bf16[1152,2048]{1,0:T(8,128)(2,1)} fusion(bf16[1152,512]{1,0:T(8,128)(2,1)} %bitcast.9, bf16[1,2048,512]{2,1,0:T(8,128)(2,1)S(1)} %copy-done), kind=kOutput, calls=%fused_computation | convolution fusion | flops 2418278400 | bytes 7995392 | tf_op jit(solution)/shard_map/dot_general | solution.py:552
  76.0 10.7 %all-to-all-done = bf16[16,72,512]{2,1,0:T(8,128)(2,1)} async-done(((bf16[16,72,512]{2,1,0:T(8,128)(2,1)}), bf16[16,72,512]{2,1,0:T(8,128)(2,1)}, u32[]{:S(2)}, u32[]{:S(2)}) %all-to-all-start) | async-done | bytes 1179680 | tf_op jit(solution)/shard_map/all_to_all | solution.py:549
  88.3 22.6 %shard_map.218 = (bf16[1152,2048]{1,0:T(8,128)(2,1)S(1)}, bf16[1152,2048]{1,0:T(8,128)(2,1)S(1)}, bf16[1152,640]{1,0:T(8,128)(2,1)}) custom-call(bf16[1152,512]{1,0:T(8,128)(2,1)} %bitcast.7.in_ref, bf16[1152,2048]{1,0:T(8,128)(2,1)} %convolution_convert_fusion.back_ref, bf16[512,2048]{1,0:T(8,128)(2,1)S(1)} %bitcast.38), custom_call_target="tpu_custom_call" | custom-call | flops 4800000000 | bytes 20000000 | tf_op jit(solution)/shard_map/pallas_call | solution.py:555
  110.8 2.2 copy-done.19
  113.0 2.2 copy-done.21
  115.3 4.2 %all-to-all-start.2 = ((bf16[16,72,640]{2,1,0:T(8,128)(2,1)}), bf16[16,72,640]{2,1,0:T(8,128)(2,1)S(1)}, u32[]{:S(2)}, u32[]{:S(2)}) async-start(bf16[16,72,640]{2,1,0:T(8,128)(2,1)} %bitcast.12), calls=%async_computation.2 | async-start | bytes 2949120 | tf_op jit(solution)/shard_map/all_to_all | solution.py:568
  119.5 7.1 %convolution_convert_fusion.2 = bf16[512,2048]{1,0:T(8,128)(2,1)} fusion(bf16[1152,512]{1,0:T(8,128)(2,1)} %bitcast.7.in_ref, bf16[1152,2048]{1,0:T(8,128)(2,1)} %copy-done.19), kind=kOutput, calls=%fused_computation.2 | convolution fusion | flops 2416967680 | bytes 7995392 | tf_op jit(solution)/shard_map/dot_general | solution.py:569
  126.6 5.5 %convolution_convert_fusion.1 = bf16[2048,512]{1,0:T(8,128)(2,1)} fusion(bf16[1152,2048]{1,0:T(8,128)(2,1)S(1)} %copy-done.22, bf16[1152,512]{1,0:T(8,128)(2,1)} %bitcast.9), kind=kOutput, calls=%fused_computation.1 | convolution fusion | flops 2416967680 | bytes 7995392 | tf_op jit(solution)/shard_map/dot_general | solution.py:570
  132.1 6.4 %all-to-all-done.2 = bf16[16,72,640]{2,1,0:T(8,128)(2,1)S(1)} async-done(((bf16[16,72,640]{2,1,0:T(8,128)(2,1)}), bf16[16,72,640]{2,1,0:T(8,128)(2,1)S(1)}, u32[]{:S(2)}, u32[]{:S(2)}) %all-to-all-start.2) | async-done | bytes 1474592 | tf_op jit(solution)/shard_map/all_to_all | solution.py:568
  139.4 2.5 shard_map.219
  143.5 3.1 collective-permute-start.2
  146.6 4.8 %collective-permute-done.2.below_ref = bf16[288,512]{1,0:T(8,128)(2,1)S(1)} collective-permute-done((bf16[288,512]{1,0:T(8,128)(2,1)}, bf16[288,512]{1,0:T(8,128)(2,1)S(1)}, u32[]{:S(2)}, u32[]{:S(2)}) %collective-permute-start.2) | collective-permute-done | bytes 294944 | tf_op jit(solution)/shard_map/ppermute | solution.py:80
  152.1 23.9 %shard_map.220 = (f32[16,144,144]{2,1,0:T(8,128)}, bf16[64,16,512]{2,1,0:T(8,128)(2,1)}, bf16[64,16,512]{2,1,0:T(8,128)(2,1)}, bf16[288,512]{1,0:T(8,128)(2,1)},...) custom-call(s32[1]{0:T(128)} %bitcast.core_ref, f32[288,512]{1,0:T(8,128)} %copy-done.17, bf16[288,512]{1,0:T(8,128)(2,1)} %copy-done.31, ...), custom_call_target="tpu_custom_call" | custom-call | flops 6000000000 | bytes 18000000 | tf_op jit(solution)/shard_map/pallas_call | solution.py:590
  176.0 3.2 collective-permute-start.3
  179.2 1.7 copy-done.2
  181.6 3.6 %shard_map.221.small_ref = f32[64,16,128]{2,1,0:T(8,128)S(1)} custom-call(f32[16,144,144]{2,1,0:T(8,128)S(1)} %copy-done.2, s32[1,384]{1,0:T(1,128)S(1)} %copy-done.13, f32[1,512]{1,0:T(1,128)S(1)} %copy-done.15, f32[1,512]{1,0:T(1,128)S(1)} %get-tuple-element.64.gain_two_ref), custom_call_target="tpu_custom_call" | custom-call | flops 400000000 | bytes 3000000 | tf_op jit(solution)/shard_map/pallas_call | solution.py:635
  186.6 9.9 %all-to-all-start.3 = ((bf16[64,16,640]{2,1,0:T(8,128)(2,1)}), bf16[64,16,640]{2,1,0:T(8,128)(2,1)S(1)}, u32[]{:S(2)}, u32[]{:S(2)}) async-start(bf16[64,16,640]{2,1,0:T(8,128)(2,1)} %shard_map.222), calls=%async_computation.3 | async-start | bytes 2621440 | tf_op jit(solution)/shard_map/all_to_all | solution.py:643
  197.6 24.0 %collective-permute-done.4 = bf16[288,512]{1,0:T(8,128)(2,1)S(1)} collective-permute-done((bf16[288,512]{1,0:T(8,128)(2,1)S(1)}, bf16[288,512]{1,0:T(8,128)(2,1)S(1)}, u32[]{:S(2)}, u32[]{:S(2)}) %collective-permute-start.4) | collective-permute-done | bytes 294944 | tf_op jit(solution)/shard_map/ppermute | solution.py:80
  223.0 6.5 %all-to-all-start.4 = ((bf16[64,16,640]{2,1,0:T(8,128)(2,1)}), bf16[64,16,640]{2,1,0:T(8,128)(2,1)S(1)}, u32[]{:S(2)}, u32[]{:S(2)}) async-start(bf16[64,16,640]{2,1,0:T(8,128)(2,1)} %shard_map.223), calls=%async_computation.4 | async-start | bytes 2621440 | tf_op jit(solution)/shard_map/all_to_all | solution.py:647
  230.2 18.7 %all-to-all-done.4.mine_ref = bf16[64,16,640]{2,1,0:T(8,128)(2,1)S(1)} async-done(((bf16[64,16,640]{2,1,0:T(8,128)(2,1)}), bf16[64,16,640]{2,1,0:T(8,128)(2,1)S(1)}, u32[]{:S(2)}, u32[]{:S(2)}) %all-to-all-start.4) | async-done | bytes 1310752 | tf_op jit(solution)/shard_map/all_to_all | solution.py:647
  248.9 3.0 collective-permute-start.5
  253.1 53.3 %all-reduce.4.cloned.1.call-done = (bf16[1,512,2048]{2,1,0:T(8,128)(2,1)}, bf16[1,2048,512]{2,1,0:T(8,128)(2,1)}) async-done(((bf16[1,512,2048]{2,1,0:T(8,128)(2,1)}, bf16[1,2048,512]{2,1,0:T(8,128)(2,1)}), (bf16[1,512,2048]{2,1,0:T(8,128)(2,1)}, bf16[1,2048,512]{2,1,0:T(8,128)(2,1)})) %all-reduce.4.cloned.1.call-update) | async-done | bytes 4194320 | tf_op jit(solution)/shard_map/psum | solution.py:572
  306.4 4.3 %reshape.217 = f32[1,512,2048]{2,1,0:T(8,128)} convert(bf16[1,512,2048]{2,1,0:T(8,128)(2,1)} %get-tuple-element.93) | non-fusion elementwise | flops 1048576 | bytes 6291456 | tf_op jit(solution)/shard_map/reshape | solution.py:668
  310.7 2.6 reshape.219
  314.2 3.6 %shard_map.224 = (f32[512,1536]{1,0:T(8,128)}, f32[512,512]{1,0:T(8,128)}, f32[64,16,128]{2,1,0:T(8,128)S(1)}) custom-call(s32[1]{0:T(128)} %bitcast.core_ref, bf16[64,16,640]{2,1,0:T(8,128)(2,1)S(1)} %all-to-all-done.4.mine_ref, bf16[64,16,640]{2,1,0:T(8,128)(2,1)} %collective-permute-done.5.other_ref), custom_call_target="tpu_custom_call" | custom-call | bytes 7000000 | tf_op jit(solution)/shard_map/pallas_call | solution.py:648
  (95 shorter events, 26.7 us)
Async XLA Ops:
  7.2 63.2 %copy-start = (bf16[1,2048,512]{2,1,0:T(8,128)(2,1)S(1)}, bf16[1,2048,512]{2,1,0:T(8,128)(2,1)}, u32[]{:S(2)}) copy-start(bf16[1,2048,512]{2,1,0:T(8,128)(2,1)} %param.25) | copy-start | bytes 6291460
  8.3 23.3 %collective-permute-start = (bf16[288,512]{1,0:T(8,128)(2,1)S(1)}, bf16[288,512]{1,0:T(8,128)(2,1)S(1)}, u32[]{:S(2)}, u32[]{:S(2)}) collective-permute-start(bf16[288,512]{1,0:T(8,128)(2,1)S(1)} %bitcast.42), channel_id=1, source_target_pairs={{0,15},{1,0},{2,1},{3,2},{4,3},{5,4},{6,5},{7,6},{8,7},{9,8},{10,9... | collective-permute-start | bytes 884744 | tf_op jit(solution)/shard_map/ppermute | solution.py:80
  19.2 7.5 %copy-start.27 = (f32[16,529]{1,0:T(8,128)S(1)}, f32[16,529]{1,0:T(8,128)}, u32[]{:S(2)}) copy-start(f32[16,529]{1,0:T(8,128)} %param.22) | copy-start | bytes 101572
  19.2 7.5 %copy-start.13 = (s32[1,384]{1,0:T(1,128)S(1)}, s32[1,384]{1,0:T(1,128)}, u32[]{:S(2)}) copy-start(s32[1,384]{1,0:T(1,128)} %constant.56.clone.targets_ref) | copy-start | bytes 4612
  22.2 43.5 %all-to-all-start.1 = ((bf16[16,72,512]{2,1,0:T(8,128)(2,1)}), bf16[16,72,512]{2,1,0:T(8,128)(2,1)}, u32[]{:S(2)}, u32[]{:S(2)}) async-start(bf16[16,72,512]{2,1,0:T(8,128)(2,1)} %bitcast.8), calls=%async_computation.1 | async-start | bytes 2359296 | tf_op jit(solution)/shard_map/all_to_all | solution.py:496
  29.4 1.4 copy-start.3
  32.4 30.0 %copy-start.14 = (f32[512]{0:T(512)S(1)}, f32[512]{0:T(512)}, u32[]{:S(2)}) copy-start(f32[512]{0:T(512)} %param.23) | copy-start | bytes 6148
  51.2 11.1 %collective-permute-start.1 = (bf16[288,512]{1,0:T(8,128)(2,1)}, bf16[288,512]{1,0:T(8,128)(2,1)S(1)}, u32[]{:S(2)}, u32[]{:S(2)}) collective-permute-start(bf16[288,512]{1,0:T(8,128)(2,1)} %get-tuple-element.43), channel_id=1, source_target_pairs={{0,1},{1,2},{2,3},{3,4},{4,5},{5,6},{6,7},{7,8},{8,9},{9,10},{10,1... | collective-permute-start | bytes 884744 | tf_op jit(solution)/shard_map/ppermute | solution.py:80
  65.8 20.9 %all-to-all-start = ((bf16[16,72,512]{2,1,0:T(8,128)(2,1)}), bf16[16,72,512]{2,1,0:T(8,128)(2,1)}, u32[]{:S(2)}, u32[]{:S(2)}) async-start(bf16[16,72,512]{2,1,0:T(8,128)(2,1)} %bitcast.33), calls=%async_computation | async-start | bytes 2359296 | tf_op jit(solution)/shard_map/all_to_all | solution.py:549
  86.7 1.6 copy-start.16
  110.8 2.2 copy-start.19
  113.0 2.2 copy-start.21
  115.3 23.2 %all-to-all-start.2 = ((bf16[16,72,640]{2,1,0:T(8,128)(2,1)}), bf16[16,72,640]{2,1,0:T(8,128)(2,1)S(1)}, u32[]{:S(2)}, u32[]{:S(2)}) async-start(bf16[16,72,640]{2,1,0:T(8,128)(2,1)} %bitcast.12), calls=%async_computation.2 | async-start | bytes 2949120 | tf_op jit(solution)/shard_map/all_to_all | solution.py:568
  119.5 7.1 %copy-start.22 = (bf16[1152,2048]{1,0:T(8,128)(2,1)S(1)}, bf16[1152,2048]{1,0:T(8,128)(2,1)}, u32[]{:S(2)}) copy-start(bf16[1152,2048]{1,0:T(8,128)(2,1)} %copy-done.21) | copy-start | bytes 14155780
  126.6 11.9 %copy-start.9 = (bf16[1,12,48,512]{3,2,1,0:T(8,128)(2,1)S(1)}, bf16[1,12,48,512]{3,2,1,0:T(8,128)(2,1)}, u32[]{:S(2)}) copy-start(bf16[1,12,48,512]{3,2,1,0:T(8,128)(2,1)} %param.16) | copy-start | bytes 1769476
  126.6 11.9 %copy-start.12 = (bf16[288,288]{1,0:T(8,128)(2,1)S(1)}, bf16[288,288]{1,0:T(8,128)(2,1)}, u32[]{:S(2)}) copy-start(bf16[288,288]{1,0:T(8,128)(2,1)} %constant.53.clone.order_ref) | copy-start | bytes 497668
  143.5 7.9 %collective-permute-start.2 = (bf16[288,512]{1,0:T(8,128)(2,1)}, bf16[288,512]{1,0:T(8,128)(2,1)S(1)}, u32[]{:S(2)}, u32[]{:S(2)}) collective-permute-start(bf16[288,512]{1,0:T(8,128)(2,1)} %get-tuple-element.54), channel_id=1, source_target_pairs={{0,15},{1,0},{2,1},{3,2},{4,3},{5,4},{6,5},{7,6},{8,7},{9,8},{10,9... | collective-permute-start | bytes 884744 | tf_op jit(solution)/shard_map/ppermute | solution.py:80
  176.0 9.2 %collective-permute-start.3 = (bf16[64,16,512]{2,1,0:T(8,128)(2,1)}, bf16[64,16,512]{2,1,0:T(8,128)(2,1)S(1)}, u32[]{:S(2)}, u32[]{:S(2)}) collective-permute-start(bf16[64,16,512]{2,1,0:T(8,128)(2,1)} %get-tuple-element.61), channel_id=1, source_target_pairs={{0,16},{16,0},{1,17},{17,1},{2,18},{18,2},{3,19},{19,3},{4,20},{20... | collective-permute-start | bytes 3145736 | tf_op jit(solution)/shard_map/ppermute | solution.py:80
  179.2 1.7 copy-start.2
  181.6 3.6 %copy-start.7 = (bf16[64,16,512]{2,1,0:T(8,128)(2,1)S(1)}, bf16[64,16,512]{2,1,0:T(8,128)(2,1)}, u32[]{:S(2)}) copy-start(bf16[64,16,512]{2,1,0:T(8,128)(2,1)} %get-tuple-element.60.mine_ref) | copy-start | bytes 3145732
  186.6 9.9 %copy-start.30 = (bf16[288,512]{1,0:T(8,128)(2,1)S(1)}, bf16[288,512]{1,0:T(8,128)(2,1)}, u32[]{:S(2)}) copy-start(bf16[288,512]{1,0:T(8,128)(2,1)} %get-tuple-element.65) | copy-start | bytes 884740
  186.6 35.0 %all-to-all-start.3 = ((bf16[64,16,640]{2,1,0:T(8,128)(2,1)}), bf16[64,16,640]{2,1,0:T(8,128)(2,1)S(1)}, u32[]{:S(2)}, u32[]{:S(2)}) async-start(bf16[64,16,640]{2,1,0:T(8,128)(2,1)} %shard_map.222), calls=%async_computation.3 | async-start | bytes 2621440 | tf_op jit(solution)/shard_map/all_to_all | solution.py:643
  196.5 25.1 %collective-permute-start.4 = (bf16[288,512]{1,0:T(8,128)(2,1)S(1)}, bf16[288,512]{1,0:T(8,128)(2,1)S(1)}, u32[]{:S(2)}, u32[]{:S(2)}) collective-permute-start(bf16[288,512]{1,0:T(8,128)(2,1)S(1)} %copy-done.30), channel_id=1, source_target_pairs={{0,1},{1,2},{2,3},{3,4},{4,5},{5,6},{6,7},{7,8},{8,9},{9,10},{10,1... | collective-permute-start | bytes 884744 | tf_op jit(solution)/shard_map/ppermute | solution.py:80
  223.0 26.0 %all-to-all-start.4 = ((bf16[64,16,640]{2,1,0:T(8,128)(2,1)}), bf16[64,16,640]{2,1,0:T(8,128)(2,1)S(1)}, u32[]{:S(2)}, u32[]{:S(2)}) async-start(bf16[64,16,640]{2,1,0:T(8,128)(2,1)} %shard_map.223), calls=%async_computation.4 | async-start | bytes 2621440 | tf_op jit(solution)/shard_map/all_to_all | solution.py:647
  229.5 76.9 %all-reduce.4.cloned.1.call-start = ((), (), s32[]{:S(2)}) async-start(), calls=%async_computation.5 | async-start | bytes 8388608 | tf_op jit(solution)/shard_map/psum | solution.py:572
  229.5 22.3 %copy-start.6 = (f32[576,128]{1,0:T(8,128)S(1)}, f32[576,128]{1,0:T(8,128)}, u32[]{:S(2)}) copy-start(f32[576,128]{1,0:T(8,128)} %copy-done.5) | copy-start | bytes 884740
  229.5 22.9 %copy-start.28 = (bf16[1,12,48]{2,1,0:T(8,128)(2,1)S(1)}, bf16[1,12,48]{2,1,0:T(8,128)(2,1)}, u32[]{:S(2)}) copy-start(bf16[1,12,48]{2,1,0:T(8,128)(2,1)} %param.17) | copy-start | bytes 3460
  248.9 65.2 %collective-permute-start.5 = (bf16[64,16,640]{2,1,0:T(8,128)(2,1)S(1)}, bf16[64,16,640]{2,1,0:T(8,128)(2,1)}, u32[]{:S(2)}, u32[]{:S(2)}) collective-permute-start(bf16[64,16,640]{2,1,0:T(8,128)(2,1)S(1)} %all-to-all-done.4.mine_ref), channel_id=1, source_target_pairs={{0,16},{16,0},{1,17},{17,1},{2,18},{18,2},{3,19},{19,3},{4,20},{20... | collective-permute-start | bytes 3932168 | tf_op jit(solution)/shard_map/ppermute | solution.py:80
  306.4 4.3 %copy-start.23 = (bf16[1,2048,512]{2,1,0:T(8,128)(2,1)S(1)}, bf16[1,2048,512]{2,1,0:T(8,128)(2,1)}, u32[]{:S(2)}) copy-start(bf16[1,2048,512]{2,1,0:T(8,128)(2,1)} %get-tuple-element.94) | copy-start | bytes 6291460
  310.7 2.6 copy-start.24
  310.7 2.6 copy-start.26
  310.7 8.3 %copy-start.1 = (bf16[1,2048,512]{2,1,0:T(8,128)(2,1)S(1)}, bf16[1,2048,512]{2,1,0:T(8,128)(2,1)}, u32[]{:S(2)}) copy-start(bf16[1,2048,512]{2,1,0:T(8,128)(2,1)} %param.25) | copy-start | bytes 6291460
  (12 other events, 10.9 us)
Sparse Core Ops, SparseCore 0:
  233.3 73.0 all-reduce.3
